TPU v7x, 32 devices: a whole 2x2x4 slice. The times are simulated.
32 devices in a mesh: wide: 8 (over y, x, core), narrow: 4 (over z).
Axes of the slice: x: 2, y: 2, z: 4, core: 2. Of those that a mesh axis runs over, the one named last changes fastest.
Arguments:
- x_zero: bfloat16 [4608, 3456], P(('wide', 'narrow')), may hold values from -6 to 6
- labels: int32 [4608], P(('wide', 'narrow')), may hold values 0 or 1
- cross_u: bfloat16 [3456, 256], replicated, may hold values from -0.375 to 0.375
- cross_v: bfloat16 [3456, 256], replicated, may hold values from -0.109375 to 0.109375
- cross_bias: float32 [3456], replicated, may hold values from -3 to 3
- head: float32 [3456], replicated, may hold values from -0.109375 to 0.109375
- hot_table: float32 [8192, 128], replicated, may hold values from -6 to 6
- hot_acc: float32 [8192], replicated, may hold values from 0.01 to 100
- cold_table: float32 [65536, 128], P(('wide', 'narrow')), may hold values from -6 to 6
- cold_acc: float32 [65536], P(('wide', 'narrow')), may hold values from 0.0001 to 0.01
- hot_ids: int32 [4608, 26, 19], P(('wide', 'narrow')), may hold values from 0 to 8191
- cold_owner: int32 [4608, 26, 1], P(('wide', 'narrow')), may hold values from 0 to 31; in each aligned block of 3744 rows (0 to 3743, 3744 to 7487, ..., all dimensions but the last counted through in order) at most 468 rows name the same one
- cold_slot: int32 [4608, 26], P(('wide', 'narrow')), may hold values from 0 to 2047
Outputs:
- hot_out: float32 [8192, 128], replicated
- cold_out: float32 [65536, 128], P(('wide', 'narrow'))
- grad_u: bfloat16 [3456, 256], replicated
- grad_v: bfloat16 [3456, 256], replicated
- grad_bias: float32 [3456], replicated
Inputs may be any that keep to these rules, and one draw needn't show every extreme that they name: `cold_owner`: an owner is a device's index over wide and narrow, wide slowest. Among the 3744 bags of one device no owner is named by more than 468 bags, a bound that some block reaches.
All inputs are finite; a program needn't handle non-finite values. No bound on the sum of `labels` on one device may be relied on, other than what follows from the above.
Results may differ from a plain program's by a relative error of at most 0.0058.
Values may be sent and summed in bfloat16 or wider, within the bound.
A program may use at most 128 MiB of HBM per device.

v0:
```python
import math
import jax
import jax.numpy as jnp
from jax import lax
from jax.sharding import PartitionSpec as P

LEARN_RATE = 0.5
EPSILON = 1e-08


def adagrad_rows(table, accum, grad):
    new_acc = accum + jnp.mean(grad * grad, axis=1)
    return table - LEARN_RATE * grad / (jnp.sqrt(new_acc)[:, None] + EPSILON)


def per_device(
    x_zero,
    labels,
    cross_u,
    cross_v,
    cross_bias,
    head,
    hot_table,
    hot_acc,
    cold_table,
    cold_acc,
    hot_ids,
    cold_owner,
    cold_slot,
):
    samples = x_zero.shape[0]
    emb_width = cold_table.shape[1]
    features = hot_ids.shape[1]
    lanes = hot_ids.shape[2]
    shard_rows = cold_table.shape[0]
    hot_rows_all = hot_table.shape[0]
    bag_count = samples * features
    proj_b = jnp.dot(x_zero, cross_v, preferred_element_type=jnp.float32).astype(jnp.bfloat16)
    mixed = jnp.dot(proj_b, cross_u.T, preferred_element_type=jnp.float32)
    scale = mixed + cross_bias[None, :]
    x_float = x_zero.astype(jnp.float32)
    crossed = x_float * scale + x_float
    logit = jnp.sum(crossed * head[None, :], axis=1)
    delta = jax.nn.sigmoid(logit) - labels.astype(jnp.float32)
    upstream = delta[:, None] * head[None, :]
    dscale = upstream * x_float
    dscale_b = dscale.astype(jnp.bfloat16)
    dproj_b = jnp.dot(dscale_b, cross_u, preferred_element_type=jnp.float32).astype(jnp.bfloat16)
    pooled = upstream[:, emb_width:] * (scale[:, emb_width:] + 1.0) + jnp.dot(
        dproj_b, cross_v[emb_width:].T, preferred_element_type=jnp.float32
    )
    flat_b = pooled.astype(jnp.bfloat16).reshape(bag_count, emb_width)
    owners = cold_owner.reshape(bag_count)
    places = cold_slot.reshape(bag_count)
    devices = lax.axis_size(("wide", "narrow"))
    capacity = 4 * bag_count // devices
    order = jnp.argsort(owners, stable=True)
    sorted_owner = owners[order]
    counts = jnp.sum(
        (owners[:, None] == jnp.arange(devices, dtype=jnp.int32)[None, :]).astype(jnp.int32), axis=0
    )
    starts = jnp.cumsum(counts) - counts
    position = jnp.arange(bag_count, dtype=jnp.int32) - starts[sorted_owner]
    target = sorted_owner * capacity + position
    send_grad = (
        jnp.zeros((devices * capacity, emb_width), jnp.bfloat16).at[target].set(flat_b[order])
    )
    send_place = jnp.zeros((devices * capacity,), jnp.int32).at[target].set(places[order])
    recv_grad, recv_place = (
        lax.all_to_all(
            send_grad.reshape(devices, capacity, emb_width),
            ("wide", "narrow"),
            split_axis=0,
            concat_axis=0,
            tiled=True,
        ),
        lax.all_to_all(
            send_place.reshape(devices, capacity),
            ("wide", "narrow"),
            split_axis=0,
            concat_axis=0,
            tiled=True,
        ),
    )
    recv_rows = recv_grad.reshape(-1, emb_width)
    recv_where = recv_place.reshape(-1)
    slot_block = math.gcd(shard_rows, 512)

    def cold_block(first):
        columns = first + jnp.arange(slot_block, dtype=jnp.int32)
        onehot = (recv_where[:, None] == columns[None, :]).astype(jnp.bfloat16)
        return lax.dot_general(
            onehot, recv_rows, (((0,), (0,)), ((), ())), preferred_element_type=jnp.float32
        )

    cold_firsts = jnp.arange(0, shard_rows, slot_block, dtype=jnp.int32)
    cold_grad = lax.map(cold_block, cold_firsts).reshape(shard_rows, emb_width)
    cold_out = adagrad_rows(cold_table, cold_acc, cold_grad)
    flat_ids = hot_ids.reshape(bag_count, lanes)
    hot_block = math.gcd(hot_rows_all, 1024)

    def hot_part(first):
        columns = first + jnp.arange(hot_block, dtype=jnp.int32)
        tally = jnp.zeros((bag_count, hot_block), jnp.bfloat16)
        for lane in range(lanes):
            tally = tally + (flat_ids[:, lane][:, None] == columns[None, :]).astype(jnp.bfloat16)
        return lax.dot_general(
            tally, flat_b, (((0,), (0,)), ((), ())), preferred_element_type=jnp.float32
        )

    hot_firsts = jnp.arange(0, hot_rows_all, hot_block, dtype=jnp.int32)
    hot_local = lax.map(hot_part, hot_firsts).reshape(hot_rows_all, emb_width)
    part_u = lax.dot_general(
        dscale_b, proj_b, (((0,), (0,)), ((), ())), preferred_element_type=jnp.float32
    )
    part_v = lax.dot_general(
        x_zero, dproj_b, (((0,), (0,)), ((), ())), preferred_element_type=jnp.float32
    )
    part_c = jnp.sum(dscale, axis=0)
    hot_grad, sum_u, sum_v, sum_c = lax.psum(
        (hot_local, part_u, part_v, part_c), ("wide", "narrow")
    )
    hot_out = adagrad_rows(hot_table, hot_acc, hot_grad)
    return (hot_out, cold_out, sum_u.astype(jnp.bfloat16), sum_v.astype(jnp.bfloat16), sum_c)


def solution(mesh):
    placed = (
        P(("wide", "narrow"), None),
        P(("wide", "narrow")),
        P(),
        P(),
        P(),
        P(),
        P(),
        P(),
        P(("wide", "narrow"), None),
        P(("wide", "narrow")),
        P(("wide", "narrow"), None, None),
        P(("wide", "narrow"), None, None),
        P(("wide", "narrow"), None),
    )
    return jax.shard_map(
        per_device,
        mesh=mesh,
        in_specs=placed,
        out_specs=(P(), P(("wide", "narrow"), None), P(), P(), P()),
        check_vma=False,
    )
```

profile of v0, /device:TPU:0, one launch (start us, length us, event | category | flops | bytes accessed | tf_op | source)
XLA Modules:
  0.0 670.6 jit_solution(11999604817901376762)
XLA Ops:
  7.2 1.0 copy.32
  10.2 5.8 sort.17
  16.0 19.9 %gather_fusion = s32[3744]{0:T(1024)S(1)} fusion(s32[3744]{0:T(1024)S(1)} %reshape.130, s32[4096]{0:T(1024)S(1)} %pad_clamp_fusion), kind=kCustom, calls=%fused_computation | custom fusion | bytes 44928 | tf_op jit(solution)/shard_map/gather | solution.py:58
  36.2 19.9 %gather_fusion.1 = s32[3744]{0:T(1024)S(1)} fusion(s32[3744]{0:T(1024)S(1)} %reshape.133, s32[4096]{0:T(1024)S(1)} %pad_clamp_fusion), kind=kCustom, calls=%fused_computation.1 | custom fusion | bytes 44928 | tf_op jit(solution)/shard_map/gather | solution.py:68
  56.1 4.4 fusion.71
  60.5 1.1 compare_reduce_fusion.24
  61.6 15.8 %select_select_fusion = s32[3744]{0:T(1024)S(1)} fusion(pred[3744]{0:T(1024)(128)(4,1)S(1)} %get-tuple-element.126, pred[3744]{0:T(1024)(128)(4,1)S(1)} %get-tuple-element.125, pred[3744]{0:T(1024)(128)(4,1)S(1)} %get-tuple-element.124, pred[3744]{0:T(1024)(128)(4,1)S(1)} %get-tuple-element.123, pred[3744]{0:T(1024)(128)(4,1)S(1)} %get-tuple-element.122, ...), kind=kLoop, calls=%fused_computation.158 | loop fusion | flops 93600 | bytes 123652 | tf_op jit(solution)/shard_map/gather | solution.py:63
  77.5 18.2 %scatter_custom_fusion = s32[14976]{0:T(1024)S(1)} fusion(s32[3744]{0:T(1024)S(1)} %fusion.72, s32[3744]{0:T(1024)S(1)} %gather_fusion.1, s32[]{:T(128)} %copy.60), kind=kCustom, calls=%fused_computation.155 | custom fusion | bytes 59908 | tf_op jit(solution)/shard_map/scatter | solution.py:68
  95.7 0.8 all_to_all.11
  96.5 7.9 %all-to-all-start = ((s32[32,1,468]{2,1,0:T(1,128)}), s32[32,1,468]{2,1,0:T(1,128)}, u32[]{:S(2)}, u32[]{:S(2)}) async-start(s32[32,1,468]{2,1,0:T(1,128)} %all_to_all.11), calls=%async_computation | async-start | bytes 131072 | tf_op jit(solution)/shard_map/all_to_all | solution.py:77
  104.4 1.9 convolution_convert_fusion.1
  106.4 0.9 fusion.57
  107.9 1.0 fusion.62
  108.8 1.7 fusion.55
  110.6 1.6 copy.31
  112.8 2.3 reshape.128
  115.1 30.2 %scatter_custom_fusion.1 = bf16[14976,128]{1,0:T(8,128)(2,1)} fusion(s32[3744]{0:T(1024)} %copy-done.17, bf16[]{:T(256)} %constant.18.clone.1, bf16[3744,128]{1,0:T(8,128)(2,1)S(1)} %reshape.128, s32[4096]{0:T(1024)S(1)} %pad_clamp_fusion), kind=kCustom, calls=%fused_computation.103 | custom fusion | bytes 3834368 | tf_op jit(solution)/shard_map/scatter | solution.py:66
  145.3 5.8 reshape.134
  151.1 6.1 all-to-all-start.1
  157.4 267.2 %while.21 = (s32[]{:T(128)}, f32[8,1024,128]{2,1,0:T(8,128)}, s32[3744,19]{0,1:T(8,128)S(1)}, s32[8]{0:T(128)S(1)}, bf16[3744,128]{1,0:T(8,128)(2,1)S(1)}, /*index=5*/s32[]{:T(128)}) while((s32[]{:T(128)}, f32[8,1024,128]{2,1,0:T(8,128)}, s32[3744,19]{0,1:T(8,128)S(1)}, s32[8]{0:T(128)S(1)}, bf16[3744,128]{1,0:T(8,128)(2,1)S(1)}, ...), condition=%wide.region_2.3_spmd, body=%wide.region_1.0_spmd.sunk | while | flops 1196164096 | bytes 2344673 | solution.py:112
  158.6 0.8 slice_reduce_fusion.20
  159.4 31.4 %fusion.100 = f32[8,1024,128]{2,1,0:T(8,128)} fusion(f32[8,1024,128]{2,1,0:T(8,128)} %get-tuple-element.323, s32[]{:T(128)S(6)} %copy.44, bf16[3744,128]{1,0:T(8,128)(2,1)S(1)} %get-tuple-element.332, s32[1024]{0:T(1024)S(1)} %iota_add_fusion.5, s32[3744]{0:T(1024)S(1)} %get-tuple-element.291, s32[3744]{0:T(1024)S(1)} %get-tuple-element.292, ...), kind=kOutput, calls=%fused_computation.70.clone.2 | convolution fusion | flops 1196163072 | bytes 1771396 | tf_op jit(solution)/shard_map/while/body/eval_jaxpr/dot_general | solution.py:107
  192.0 0.8 slice_reduce_fusion.20
  192.8 31.4 %fusion.100 = f32[8,1024,128]{2,1,0:T(8,128)} fusion(f32[8,1024,128]{2,1,0:T(8,128)} %get-tuple-element.323, s32[]{:T(128)S(6)} %copy.44, bf16[3744,128]{1,0:T(8,128)(2,1)S(1)} %get-tuple-element.332, s32[1024]{0:T(1024)S(1)} %iota_add_fusion.5, s32[3744]{0:T(1024)S(1)} %get-tuple-element.291, s32[3744]{0:T(1024)S(1)} %get-tuple-element.292, ...), kind=kOutput, calls=%fused_computation.70.clone.2 | convolution fusion | flops 1196163072 | bytes 1771396 | tf_op jit(solution)/shard_map/while/body/eval_jaxpr/dot_general | solution.py:107
  226.2 31.4 %fusion.100 = f32[8,1024,128]{2,1,0:T(8,128)} fusion(f32[8,1024,128]{2,1,0:T(8,128)} %get-tuple-element.323, s32[]{:T(128)S(6)} %copy.44, bf16[3744,128]{1,0:T(8,128)(2,1)S(1)} %get-tuple-element.332, s32[1024]{0:T(1024)S(1)} %iota_add_fusion.5, s32[3744]{0:T(1024)S(1)} %get-tuple-element.291, s32[3744]{0:T(1024)S(1)} %get-tuple-element.292, ...), kind=kOutput, calls=%fused_computation.70.clone.2 | convolution fusion | flops 1196163072 | bytes 1771396 | tf_op jit(solution)/shard_map/while/body/eval_jaxpr/dot_general | solution.py:107
  259.6 31.4 %fusion.100 = f32[8,1024,128]{2,1,0:T(8,128)} fusion(f32[8,1024,128]{2,1,0:T(8,128)} %get-tuple-element.323, s32[]{:T(128)S(6)} %copy.44, bf16[3744,128]{1,0:T(8,128)(2,1)S(1)} %get-tuple-element.332, s32[1024]{0:T(1024)S(1)} %iota_add_fusion.5, s32[3744]{0:T(1024)S(1)} %get-tuple-element.291, s32[3744]{0:T(1024)S(1)} %get-tuple-element.292, ...), kind=kOutput, calls=%fused_computation.70.clone.2 | convolution fusion | flops 1196163072 | bytes 1771396 | tf_op jit(solution)/shard_map/while/body/eval_jaxpr/dot_general | solution.py:107
  292.2 0.8 slice_reduce_fusion.20
  293.0 31.4 %fusion.100 = f32[8,1024,128]{2,1,0:T(8,128)} fusion(f32[8,1024,128]{2,1,0:T(8,128)} %get-tuple-element.323, s32[]{:T(128)S(6)} %copy.44, bf16[3744,128]{1,0:T(8,128)(2,1)S(1)} %get-tuple-element.332, s32[1024]{0:T(1024)S(1)} %iota_add_fusion.5, s32[3744]{0:T(1024)S(1)} %get-tuple-element.291, s32[3744]{0:T(1024)S(1)} %get-tuple-element.292, ...), kind=kOutput, calls=%fused_computation.70.clone.2 | convolution fusion | flops 1196163072 | bytes 1771396 | tf_op jit(solution)/shard_map/while/body/eval_jaxpr/dot_general | solution.py:107
  325.6 0.8 slice_reduce_fusion.20
  326.4 31.4 %fusion.100 = f32[8,1024,128]{2,1,0:T(8,128)} fusion(f32[8,1024,128]{2,1,0:T(8,128)} %get-tuple-element.323, s32[]{:T(128)S(6)} %copy.44, bf16[3744,128]{1,0:T(8,128)(2,1)S(1)} %get-tuple-element.332, s32[1024]{0:T(1024)S(1)} %iota_add_fusion.5, s32[3744]{0:T(1024)S(1)} %get-tuple-element.291, s32[3744]{0:T(1024)S(1)} %get-tuple-element.292, ...), kind=kOutput, calls=%fused_computation.70.clone.2 | convolution fusion | flops 1196163072 | bytes 1771396 | tf_op jit(solution)/shard_map/while/body/eval_jaxpr/dot_general | solution.py:107
  359.8 31.4 %fusion.100 = f32[8,1024,128]{2,1,0:T(8,128)} fusion(f32[8,1024,128]{2,1,0:T(8,128)} %get-tuple-element.323, s32[]{:T(128)S(6)} %copy.44, bf16[3744,128]{1,0:T(8,128)(2,1)S(1)} %get-tuple-element.332, s32[1024]{0:T(1024)S(1)} %iota_add_fusion.5, s32[3744]{0:T(1024)S(1)} %get-tuple-element.291, s32[3744]{0:T(1024)S(1)} %get-tuple-element.292, ...), kind=kOutput, calls=%fused_computation.70.clone.2 | convolution fusion | flops 1196163072 | bytes 1771396 | tf_op jit(solution)/shard_map/while/body/eval_jaxpr/dot_general | solution.py:107
  393.2 31.4 %fusion.100 = f32[8,1024,128]{2,1,0:T(8,128)} fusion(f32[8,1024,128]{2,1,0:T(8,128)} %get-tuple-element.323, s32[]{:T(128)S(6)} %copy.44, bf16[3744,128]{1,0:T(8,128)(2,1)S(1)} %get-tuple-element.332, s32[1024]{0:T(1024)S(1)} %iota_add_fusion.5, s32[3744]{0:T(1024)S(1)} %get-tuple-element.291, s32[3744]{0:T(1024)S(1)} %get-tuple-element.292, ...), kind=kOutput, calls=%fused_computation.70.clone.2 | convolution fusion | flops 1196163072 | bytes 1771396 | tf_op jit(solution)/shard_map/while/body/eval_jaxpr/dot_general | solution.py:107
  424.7 1.1 copy-done.2
  425.8 2.6 fusion.66
  428.4 2.5 convolution_bitcast_fusion
  430.9 156.5 %all-reduce.5 = (bf16[3456,256]{1,0:T(8,128)(2,1)}, bf16[3456,256]{0,1:T(8,128)(2,1)S(1)}, f32[3456]{0:T(1024)}) all-reduce(f32[3456,256]{1,0:T(8,128)} %fusion.66, f32[3456,256]{0,1:T(8,128)} %convolution_bitcast_fusion, f32[3456]{0:T(1024)S(1)} %copy-done.13), channel_id=1, replica_groups=mesh['wide'=8,'narrow'=4] {'wide','narrow'}, use_global_device_ids=true, to_apply=%region_13.14 | all-reduce | flops 1772928 | bytes 10644480 | tf_op jit(solution)/shard_map/psum | solution.py:120
  587.4 2.2 copy.35
  589.6 0.9 copy.39
  590.7 3.5 multiply_reduce_fusion
  594.2 4.2 divide_subtract_fusion
  598.4 5.8 reshape.135
  604.3 56.4 %while.22 = (s32[]{:T(128)}, f32[4,512,128]{2,1,0:T(8,128)}, s32[32,468]{1,0:T(8,128)}, s32[4]{0:T(128)S(1)}, bf16[14976,128]{1,0:T(8,128)(2,1)}, /*index=5*/s32[14976]{0:T(1024)S(1)}, s32[]{:T(128)}) while((s32[]{:T(128)}, f32[4,512,128]{2,1,0:T(8,128)}, s32[32,468]{1,0:T(8,128)}, s32[4]{0:T(128)S(1)}, ...), condition=%wide.wide.region_11.12_spmd, body=%wide.wide.region_10.11_spmd.sunk | while | flops 1970602496 | bytes 4160105 | solution.py:97
  605.6 12.9 %fusion.103 = f32[4,512,128]{2,1,0:T(8,128)} fusion(f32[4,512,128]{2,1,0:T(8,128)} %get-tuple-element.342, s32[]{:T(128)S(6)} %copy.51, bf16[14976,128]{1,0:T(8,128)(2,1)} %get-tuple-element.352, s32[512]{0:T(512)S(1)} %iota_add_fusion.6, s32[14976]{0:T(1024)S(1)} %get-tuple-element.353), kind=kOutput, calls=%fused_computation.10.clone.clone.1 | convolution fusion | flops 1970601984 | bytes 4157956 | tf_op jit(solution)/shard_map/while/body/eval_jaxpr/dot_general | solution.py:92
  619.6 12.9 %fusion.103 = f32[4,512,128]{2,1,0:T(8,128)} fusion(f32[4,512,128]{2,1,0:T(8,128)} %get-tuple-element.342, s32[]{:T(128)S(6)} %copy.51, bf16[14976,128]{1,0:T(8,128)(2,1)} %get-tuple-element.352, s32[512]{0:T(512)S(1)} %iota_add_fusion.6, s32[14976]{0:T(1024)S(1)} %get-tuple-element.353), kind=kOutput, calls=%fused_computation.10.clone.clone.1 | convolution fusion | flops 1970601984 | bytes 4157956 | tf_op jit(solution)/shard_map/while/body/eval_jaxpr/dot_general | solution.py:92
  633.7 12.9 %fusion.103 = f32[4,512,128]{2,1,0:T(8,128)} fusion(f32[4,512,128]{2,1,0:T(8,128)} %get-tuple-element.342, s32[]{:T(128)S(6)} %copy.51, bf16[14976,128]{1,0:T(8,128)(2,1)} %get-tuple-element.352, s32[512]{0:T(512)S(1)} %iota_add_fusion.6, s32[14976]{0:T(1024)S(1)} %get-tuple-element.353), kind=kOutput, calls=%fused_computation.10.clone.clone.1 | convolution fusion | flops 1970601984 | bytes 4157956 | tf_op jit(solution)/shard_map/while/body/eval_jaxpr/dot_general | solution.py:92
  647.7 12.9 %fusion.103 = f32[4,512,128]{2,1,0:T(8,128)} fusion(f32[4,512,128]{2,1,0:T(8,128)} %get-tuple-element.342, s32[]{:T(128)S(6)} %copy.51, bf16[14976,128]{1,0:T(8,128)(2,1)} %get-tuple-element.352, s32[512]{0:T(512)S(1)} %iota_add_fusion.6, s32[14976]{0:T(1024)S(1)} %get-tuple-element.353), kind=kOutput, calls=%fused_computation.10.clone.clone.1 | convolution fusion | flops 1970601984 | bytes 4157956 | tf_op jit(solution)/shard_map/while/body/eval_jaxpr/dot_general | solution.py:92
  660.6 1.6 multiply_reduce_fusion.1
  662.2 1.3 fusion.64
  (102 shorter events, 21.3 us)
Async XLA Ops:
  7.2 99.2 %copy-start = (bf16[3456,256]{1,0:T(8,128)(2,1)S(1)}, bf16[3456,256]{1,0:T(8,128)(2,1)}, u32[]{:S(2)}) copy-start(bf16[3456,256]{1,0:T(8,128)(2,1)} %param.19) | copy-start | bytes 5308420
  16.0 19.9 %copy-start.15 = (s32[144,26]{0,1:T(8,128)S(1)}, s32[144,26]{0,1:T(8,128)}, u32[]{:S(2)}) copy-start(s32[144,26]{0,1:T(8,128)} %param.29) | copy-start | bytes 44932
  36.2 68.2 %copy-start.1 = (bf16[144,3456]{1,0:T(8,128)(2,1)S(1)}, bf16[144,3456]{1,0:T(8,128)(2,1)}, u32[]{:S(2)}) copy-start(bf16[144,3456]{1,0:T(8,128)(2,1)} %param.17) | copy-start | bytes 2985988
  36.2 70.2 %copy-start.11 = (f32[3456]{0:T(1024)S(1)}, f32[3456]{0:T(1024)}, u32[]{:S(2)}) copy-start(f32[3456]{0:T(1024)} %param.22) | copy-start | bytes 41476
  36.2 70.2 %copy-start.16 = (f32[3456]{0:T(1024)S(1)}, f32[3456]{0:T(1024)}, u32[]{:S(2)}) copy-start(f32[3456]{0:T(1024)} %param.21) | copy-start | bytes 41476
  77.5 29.8 %copy-start.17 = (s32[3744]{0:T(1024)}, s32[3744]{0:T(1024)S(1)}, u32[]{:S(2)}) copy-start(s32[3744]{0:T(1024)S(1)} %fusion.72) | copy-start | bytes 44932
  96.5 54.6 %all-to-all-start = ((s32[32,1,468]{2,1,0:T(1,128)}), s32[32,1,468]{2,1,0:T(1,128)}, u32[]{:S(2)}, u32[]{:S(2)}) async-start(s32[32,1,468]{2,1,0:T(1,128)} %all_to_all.11), calls=%async_computation | async-start | bytes 131072 | tf_op jit(solution)/shard_map/all_to_all | solution.py:77
  104.4 2.9 copy-start.21
  106.4 1.5 copy-start.6
  107.3 1.6 copy-start.4
  107.3 3.2 copy-start.18
  107.9 1.0 copy-start.8
  151.1 447.3 %all-to-all-start.1 = ((bf16[32,468,128]{2,1,0:T(8,128)(2,1)}), bf16[32,468,128]{2,1,0:T(8,128)(2,1)}, u32[]{:S(2)}, u32[]{:S(2)}) async-start(bf16[32,468,128]{2,1,0:T(8,128)(2,1)} %reshape.134), calls=%async_computation.1 | async-start | bytes 7733248 | tf_op jit(solution)/shard_map/all_to_all | solution.py:70
  157.2 433.5 %all-reduce.4.cloned.1.call-start = ((), (), s32[]{:S(2)}) async-start(), calls=%async_computation.2 | async-start | bytes 8388608 | tf_op jit(solution)/shard_map/psum | solution.py:120
  424.6 1.2 copy-start.2
  424.6 1.2 copy-start.7
  424.6 1.2 copy-start.12
  424.6 1.2 copy-start.19
  424.6 3.8 copy-start.9
  425.8 5.1 copy-start.13
  589.6 4.5 copy-start.14
  590.5 7.9 %copy-start.10 = (s32[32,1,468]{2,0,1:T(8,128)}, s32[32,1,468]{2,0,1:T(8,128)S(1)}, u32[]{:S(2)}) copy-start(s32[32,1,468]{2,0,1:T(8,128)S(1)} %copy.39) | copy-start | bytes 179716
  590.6 3.5 copy-start.3
  604.2 58.0 %copy-start.20 = (f32[2048]{0:T(1024)S(1)}, f32[2048]{0:T(1024)}, u32[]{:S(2)}) copy-start(f32[2048]{0:T(1024)} %param.26) | copy-start | bytes 24580
  604.2 58.0 %copy-start.5 = (f32[2048,128]{1,0:T(8,128)S(1)}, f32[2048,128]{1,0:T(8,128)}, u32[]{:S(2)}) copy-start(f32[2048,128]{1,0:T(8,128)} %param.25) | copy-start | bytes 3145732
Sparse Core Ops, SparseCore 0:
  424.8 151.6 all-reduce.3
where the time goes:
time: 677 us; the launch traced here: 671 us
  matrix products  313 us (46%)
  blocking collectives  156 us (23%)
  local copies, waits for them, and re-layouts  125 us (18%)
  other arithmetic  46.6 us (7%)
  between operations  14.7 us (2%)
  starting transfers between devices  14.2 us (2%)
    dot_general x8, matrix products, hot_part(): lax.dot_general(tally, flat_b, (((0,), (0,)), ((), ())), preferred_elemen...  251 us
    psum x1, blocking collectives, per_device(): lax.psum((hot_local, part_u, part_v, part_c), ('wide', 'narrow'))  156 us
    dot_general x4, matrix products, cold_block(): lax.dot_general(onehot, recv_rows, (((0,), (0,)), ((), ())), preferred_el...  51.6 us
    scatter x1, local copies, waits for them, and re-layouts, per_device(): jnp.zeros((devices * capacity, emb_width), jnp.bfloat16).at[target]  30.2 us
    gather x3, other arithmetic, per_device(): position = jnp.arange(bag_count, dtype=jnp.int32) - starts[sorted_owner]  21.3 us
    gather x1, local copies, waits for them, and re-layouts, per_device(): sorted_owner = owners[order]  19.9 us
    gather x1, local copies, waits for them, and re-layouts, per_device(): places[order]  19.9 us
    scatter x1, local copies, waits for them, and re-layouts, per_device(): jnp.zeros((devices * capacity,), jnp.int32).at[target].set(places[order])  18.2 us
  transfers between devices with their start and end apart: 3, of which 0 were waited for; matrix products, arithmetic and copies ran while one was open for 49% of the time, Pallas kernels for 0%

commit v1 on v0

--- a/solution.py
+++ b/solution.py
@@ -1,3 +1,4 @@
+import functools
 import math
 import jax
 import jax.numpy as jnp
@@ -6,6 +7,14 @@
 
 LEARN_RATE = 0.5
 EPSILON = 1e-08
+
+
+def show_the_loads(matrix, shard_axis, axis_id):
+    field_out = lax.psum(matrix, axis_name=shard_axis)
+    return lax.psum(field_out, axis_id)
+
+
+test_spots = functools.partial(show_the_loads, shard_axis="narrow", axis_id="wide")
 
 
 def adagrad_rows(table, accum, grad):
@@ -117,9 +126,7 @@
         x_zero, dproj_b, (((0,), (0,)), ((), ())), preferred_element_type=jnp.float32
     )
     part_c = jnp.sum(dscale, axis=0)
-    hot_grad, sum_u, sum_v, sum_c = lax.psum(
-        (hot_local, part_u, part_v, part_c), ("wide", "narrow")
-    )
+    hot_grad, sum_u, sum_v, sum_c = test_spots((hot_local, part_u, part_v, part_c))
     hot_out = adagrad_rows(hot_table, hot_acc, hot_grad)
     return (hot_out, cold_out, sum_u.astype(jnp.bfloat16), sum_v.astype(jnp.bfloat16), sum_c)
 

time: 677 us -> 1030 us (1.52)
  waiting for transfers between devices: 0.04 us -> 302 us
  blocking collectives: 156 us -> 208 us
    psum x1 -> x2, waiting for transfers between devices: 0.02 us -> 302 us  [the longest x1 302 us: show_the_loads(): field_out = lax.psum(matrix, axis_name=shard_axis)]
    psum x1 -> x2, blocking collectives: 156 us -> 208 us  [the longest x1 188 us: show_the_loads(): return lax.psum(field_out, axis_id)]
  transfers between devices with their start and end apart: 3 -> 4, of which waited for: 0 -> 1; matrix products, arithmetic and copies ran while one was open for 49% -> 38% of each run, Pallas kernels for 0% -> 0%
where the time goes in v1:
time: 1030 us; the launch traced here: 1020 us
  matrix products  312 us (30%)
  waiting for transfers between devices  302 us (29%)
  blocking collectives  208 us (20%)
  local copies, waits for them, and re-layouts  123 us (12%)
  other arithmetic  47.2 us (5%)
  between operations  14.8 us (1%)
  starting transfers between devices  14.1 us (1%)
    psum x1, waiting for transfers between devices, show_the_loads(): field_out = lax.psum(matrix, axis_name=shard_axis)  302 us
    dot_general x8, matrix products, hot_part(): lax.dot_general(tally, flat_b, (((0,), (0,)), ((), ())), preferred_elemen...  251 us
    psum x1, blocking collectives, show_the_loads(): return lax.psum(field_out, axis_id)  188 us
    dot_general x4, matrix products, cold_block(): lax.dot_general(onehot, recv_rows, (((0,), (0,)), ((), ())), preferred_el...  51.7 us
    scatter x1, local copies, waits for them, and re-layouts, per_device(): jnp.zeros((devices * capacity, emb_width), jnp.bfloat16).at[target]  30.1 us
    gather x3, other arithmetic, per_device(): position = jnp.arange(bag_count, dtype=jnp.int32) - starts[sorted_owner]  21.3 us
  transfers between devices with their start and end apart: 4, of which 1 were waited for; matrix products, arithmetic and copies ran while one was open for 38% of the time, Pallas kernels for 0%

profile of v1, /device:TPU:0, one launch (start us, length us, event | category | flops | bytes accessed | tf_op | source)
XLA Modules:
  0.0 1021.2 jit_solution(16147189925082279091)
XLA Ops:
  7.2 1.0 copy.32
  10.2 5.8 sort.17
  16.0 19.9 %gather_fusion = s32[3744]{0:T(1024)S(1)} fusion(s32[3744]{0:T(1024)S(1)} %reshape.130, s32[4096]{0:T(1024)S(1)} %pad_clamp_fusion), kind=kCustom, calls=%fused_computation | custom fusion | bytes 44928 | tf_op jit(solution)/shard_map/gather | solution.py:67
  35.9 4.4 fusion.71
  40.3 1.1 compare_reduce_fusion.24
  41.5 15.8 %select_select_fusion = s32[3744]{0:T(1024)S(1)} fusion(pred[3744]{0:T(1024)(128)(4,1)S(1)} %get-tuple-element.126, pred[3744]{0:T(1024)(128)(4,1)S(1)} %get-tuple-element.125, pred[3744]{0:T(1024)(128)(4,1)S(1)} %get-tuple-element.124, pred[3744]{0:T(1024)(128)(4,1)S(1)} %get-tuple-element.123, pred[3744]{0:T(1024)(128)(4,1)S(1)} %get-tuple-element.122, ...), kind=kLoop, calls=%fused_computation.158 | loop fusion | flops 93600 | bytes 123652 | tf_op jit(solution)/shard_map/gather | solution.py:72
  57.6 19.9 %gather_fusion.1 = s32[3744]{0:T(1024)S(1)} fusion(s32[3744]{0:T(1024)S(1)} %reshape.133, s32[4096]{0:T(1024)S(1)} %pad_clamp_fusion), kind=kCustom, calls=%fused_computation.1 | custom fusion | bytes 44928 | tf_op jit(solution)/shard_map/gather | solution.py:77
  77.5 18.2 %scatter_custom_fusion = s32[14976]{0:T(1024)S(1)} fusion(s32[3744]{0:T(1024)S(1)} %fusion.72, s32[3744]{0:T(1024)S(1)} %gather_fusion.1, s32[]{:T(128)} %copy.63), kind=kCustom, calls=%fused_computation.155 | custom fusion | bytes 59908 | tf_op jit(solution)/shard_map/scatter | solution.py:77
  95.7 0.8 all_to_all.11
  96.5 7.8 all-to-all-start
  104.3 1.9 convolution_convert_fusion.1
  106.3 0.9 fusion.57
  107.8 1.0 fusion.62
  108.8 0.8 fusion.55
  111.0 1.2 reshape.128
  112.2 30.1 %scatter_custom_fusion.1 = bf16[14976,128]{1,0:T(8,128)(2,1)} fusion(s32[3744]{0:T(1024)S(1)} %fusion.72, bf16[]{:T(256)} %constant.18.clone.1, bf16[3744,128]{1,0:T(8,128)(2,1)S(1)} %reshape.128, s32[4096]{0:T(1024)S(1)} %pad_clamp_fusion), kind=kCustom, calls=%fused_computation.103 | custom fusion | bytes 3833858 | tf_op jit(solution)/shard_map/scatter | solution.py:75
  142.3 5.8 reshape.134
  148.8 6.1 all-to-all-start.1
  155.1 267.2 %while.21 = (s32[]{:T(128)}, f32[8,1024,128]{2,1,0:T(8,128)}, s32[3744,19]{0,1:T(8,128)S(1)}, s32[8]{0:T(128)S(1)}, bf16[3744,128]{1,0:T(8,128)(2,1)S(1)}, /*index=5*/s32[]{:T(128)}) while((s32[]{:T(128)}, f32[8,1024,128]{2,1,0:T(8,128)}, s32[3744,19]{0,1:T(8,128)S(1)}, s32[8]{0:T(128)S(1)}, bf16[3744,128]{1,0:T(8,128)(2,1)S(1)}, ...), condition=%wide.region_2.3_spmd, body=%wide.region_1.0_spmd.sunk | while | flops 1196164096 | bytes 2344673 | solution.py:121
  156.3 0.8 slice_reduce_fusion.20
  157.1 31.4 %fusion.100 = f32[8,1024,128]{2,1,0:T(8,128)} fusion(f32[8,1024,128]{2,1,0:T(8,128)} %get-tuple-element.326, s32[]{:T(128)S(6)} %copy.44, bf16[3744,128]{1,0:T(8,128)(2,1)S(1)} %get-tuple-element.335, s32[1024]{0:T(1024)S(1)} %iota_add_fusion.5, s32[3744]{0:T(1024)S(1)} %get-tuple-element.294, s32[3744]{0:T(1024)S(1)} %get-tuple-element.295, ...), kind=kOutput, calls=%fused_computation.70.clone.2 | convolution fusion | flops 1196163072 | bytes 1771396 | tf_op jit(solution)/shard_map/while/body/eval_jaxpr/dot_general | solution.py:116
  189.7 0.8 slice_reduce_fusion.20
  190.5 31.4 %fusion.100 = f32[8,1024,128]{2,1,0:T(8,128)} fusion(f32[8,1024,128]{2,1,0:T(8,128)} %get-tuple-element.326, s32[]{:T(128)S(6)} %copy.44, bf16[3744,128]{1,0:T(8,128)(2,1)S(1)} %get-tuple-element.335, s32[1024]{0:T(1024)S(1)} %iota_add_fusion.5, s32[3744]{0:T(1024)S(1)} %get-tuple-element.294, s32[3744]{0:T(1024)S(1)} %get-tuple-element.295, ...), kind=kOutput, calls=%fused_computation.70.clone.2 | convolution fusion | flops 1196163072 | bytes 1771396 | tf_op jit(solution)/shard_map/while/body/eval_jaxpr/dot_general | solution.py:116
  223.1 0.8 slice_reduce_fusion.20
  223.9 31.4 %fusion.100 = f32[8,1024,128]{2,1,0:T(8,128)} fusion(f32[8,1024,128]{2,1,0:T(8,128)} %get-tuple-element.326, s32[]{:T(128)S(6)} %copy.44, bf16[3744,128]{1,0:T(8,128)(2,1)S(1)} %get-tuple-element.335, s32[1024]{0:T(1024)S(1)} %iota_add_fusion.5, s32[3744]{0:T(1024)S(1)} %get-tuple-element.294, s32[3744]{0:T(1024)S(1)} %get-tuple-element.295, ...), kind=kOutput, calls=%fused_computation.70.clone.2 | convolution fusion | flops 1196163072 | bytes 1771396 | tf_op jit(solution)/shard_map/while/body/eval_jaxpr/dot_general | solution.py:116
  256.5 0.8 slice_reduce_fusion.20
  257.3 31.4 %fusion.100 = f32[8,1024,128]{2,1,0:T(8,128)} fusion(f32[8,1024,128]{2,1,0:T(8,128)} %get-tuple-element.326, s32[]{:T(128)S(6)} %copy.44, bf16[3744,128]{1,0:T(8,128)(2,1)S(1)} %get-tuple-element.335, s32[1024]{0:T(1024)S(1)} %iota_add_fusion.5, s32[3744]{0:T(1024)S(1)} %get-tuple-element.294, s32[3744]{0:T(1024)S(1)} %get-tuple-element.295, ...), kind=kOutput, calls=%fused_computation.70.clone.2 | convolution fusion | flops 1196163072 | bytes 1771396 | tf_op jit(solution)/shard_map/while/body/eval_jaxpr/dot_general | solution.py:116
  289.9 0.8 slice_reduce_fusion.20
  290.7 31.4 %fusion.100 = f32[8,1024,128]{2,1,0:T(8,128)} fusion(f32[8,1024,128]{2,1,0:T(8,128)} %get-tuple-element.326, s32[]{:T(128)S(6)} %copy.44, bf16[3744,128]{1,0:T(8,128)(2,1)S(1)} %get-tuple-element.335, s32[1024]{0:T(1024)S(1)} %iota_add_fusion.5, s32[3744]{0:T(1024)S(1)} %get-tuple-element.294, s32[3744]{0:T(1024)S(1)} %get-tuple-element.295, ...), kind=kOutput, calls=%fused_computation.70.clone.2 | convolution fusion | flops 1196163072 | bytes 1771396 | tf_op jit(solution)/shard_map/while/body/eval_jaxpr/dot_general | solution.py:116
  324.1 31.4 %fusion.100 = f32[8,1024,128]{2,1,0:T(8,128)} fusion(f32[8,1024,128]{2,1,0:T(8,128)} %get-tuple-element.326, s32[]{:T(128)S(6)} %copy.44, bf16[3744,128]{1,0:T(8,128)(2,1)S(1)} %get-tuple-element.335, s32[1024]{0:T(1024)S(1)} %iota_add_fusion.5, s32[3744]{0:T(1024)S(1)} %get-tuple-element.294, s32[3744]{0:T(1024)S(1)} %get-tuple-element.295, ...), kind=kOutput, calls=%fused_computation.70.clone.2 | convolution fusion | flops 1196163072 | bytes 1771396 | tf_op jit(solution)/shard_map/while/body/eval_jaxpr/dot_general | solution.py:116
  357.5 31.4 %fusion.100 = f32[8,1024,128]{2,1,0:T(8,128)} fusion(f32[8,1024,128]{2,1,0:T(8,128)} %get-tuple-element.326, s32[]{:T(128)S(6)} %copy.44, bf16[3744,128]{1,0:T(8,128)(2,1)S(1)} %get-tuple-element.335, s32[1024]{0:T(1024)S(1)} %iota_add_fusion.5, s32[3744]{0:T(1024)S(1)} %get-tuple-element.294, s32[3744]{0:T(1024)S(1)} %get-tuple-element.295, ...), kind=kOutput, calls=%fused_computation.70.clone.2 | convolution fusion | flops 1196163072 | bytes 1771396 | tf_op jit(solution)/shard_map/while/body/eval_jaxpr/dot_general | solution.py:116
  390.9 31.4 %fusion.100 = f32[8,1024,128]{2,1,0:T(8,128)} fusion(f32[8,1024,128]{2,1,0:T(8,128)} %get-tuple-element.326, s32[]{:T(128)S(6)} %copy.44, bf16[3744,128]{1,0:T(8,128)(2,1)S(1)} %get-tuple-element.335, s32[1024]{0:T(1024)S(1)} %iota_add_fusion.5, s32[3744]{0:T(1024)S(1)} %get-tuple-element.294, s32[3744]{0:T(1024)S(1)} %get-tuple-element.295, ...), kind=kOutput, calls=%fused_computation.70.clone.2 | convolution fusion | flops 1196163072 | bytes 1771396 | tf_op jit(solution)/shard_map/while/body/eval_jaxpr/dot_general | solution.py:116
  422.3 2.5 convolution_bitcast_fusion
  424.8 2.6 fusion.66
  428.1 20.1 %psum.62 = f32[3456]{0:T(1024)S(1)} all-reduce(f32[3456]{0:T(1024)S(1)} %copy-done.19), channel_id=1, replica_groups=mesh['wide'=8,'narrow'=4] {'narrow'}, use_global_device_ids=true, to_apply=%region_19.20 | all-reduce | flops 3456 | bytes 27648 | tf_op jit(solution)/shard_map/psum | solution.py:13
  448.4 5.8 reshape.135
  454.2 56.6 %while.22 = (s32[]{:T(128)}, f32[4,512,128]{2,1,0:T(8,128)}, s32[32,468]{1,0:T(8,128)}, s32[4]{0:T(128)S(1)}, bf16[14976,128]{1,0:T(8,128)(2,1)}, /*index=5*/s32[14976]{0:T(1024)S(1)}, s32[]{:T(128)}) while((s32[]{:T(128)}, f32[4,512,128]{2,1,0:T(8,128)}, s32[32,468]{1,0:T(8,128)}, s32[4]{0:T(128)S(1)}, ...), condition=%wide.wide.region_12.13_spmd, body=%wide.wide.region_11.12_spmd.sunk | while | flops 1970602496 | bytes 4160105 | solution.py:106
  455.5 12.9 %fusion.103 = f32[4,512,128]{2,1,0:T(8,128)} fusion(f32[4,512,128]{2,1,0:T(8,128)} %get-tuple-element.345, s32[]{:T(128)S(6)} %copy.54, bf16[14976,128]{1,0:T(8,128)(2,1)} %get-tuple-element.355, s32[512]{0:T(512)S(1)} %iota_add_fusion.6, s32[14976]{0:T(1024)S(1)} %get-tuple-element.356), kind=kOutput, calls=%fused_computation.10.clone.clone.1 | convolution fusion | flops 1970601984 | bytes 4157956 | tf_op jit(solution)/shard_map/while/body/eval_jaxpr/dot_general | solution.py:101
  469.6 12.9 %fusion.103 = f32[4,512,128]{2,1,0:T(8,128)} fusion(f32[4,512,128]{2,1,0:T(8,128)} %get-tuple-element.345, s32[]{:T(128)S(6)} %copy.54, bf16[14976,128]{1,0:T(8,128)(2,1)} %get-tuple-element.355, s32[512]{0:T(512)S(1)} %iota_add_fusion.6, s32[14976]{0:T(1024)S(1)} %get-tuple-element.356), kind=kOutput, calls=%fused_computation.10.clone.clone.1 | convolution fusion | flops 1970601984 | bytes 4157956 | tf_op jit(solution)/shard_map/while/body/eval_jaxpr/dot_general | solution.py:101
  483.8 12.9 %fusion.103 = f32[4,512,128]{2,1,0:T(8,128)} fusion(f32[4,512,128]{2,1,0:T(8,128)} %get-tuple-element.345, s32[]{:T(128)S(6)} %copy.54, bf16[14976,128]{1,0:T(8,128)(2,1)} %get-tuple-element.355, s32[512]{0:T(512)S(1)} %iota_add_fusion.6, s32[14976]{0:T(1024)S(1)} %get-tuple-element.356), kind=kOutput, calls=%fused_computation.10.clone.clone.1 | convolution fusion | flops 1970601984 | bytes 4157956 | tf_op jit(solution)/shard_map/while/body/eval_jaxpr/dot_general | solution.py:101
  498.0 12.9 %fusion.103 = f32[4,512,128]{2,1,0:T(8,128)} fusion(f32[4,512,128]{2,1,0:T(8,128)} %get-tuple-element.345, s32[]{:T(128)S(6)} %copy.54, bf16[14976,128]{1,0:T(8,128)(2,1)} %get-tuple-element.355, s32[512]{0:T(512)S(1)} %iota_add_fusion.6, s32[14976]{0:T(1024)S(1)} %get-tuple-element.356), kind=kOutput, calls=%fused_computation.10.clone.clone.1 | convolution fusion | flops 1970601984 | bytes 4157956 | tf_op jit(solution)/shard_map/while/body/eval_jaxpr/dot_general | solution.py:101
  510.9 1.7 multiply_reduce_fusion.1
  512.6 301.7 %all-reduce.8.cloned.1.call-done = (f32[8192,128]{1,0:T(8,128)}, f32[3456,256]{1,0:T(8,128)}, f32[3456,256]{0,1:T(8,128)}) async-done(((f32[8192,128]{1,0:T(8,128)}, f32[3456,256]{1,0:T(8,128)}, f32[3456,256]{0,1:T(8,128)}), (f32[8192,128]{1,0:T(8,128)}, f32[3456,256]{1,0:T(8,128)}, f32[3456,256]{0,1:T(8,128)})) %all-reduce.8.cloned.1.call-update) | async-done | bytes 11272208 | tf_op jit(solution)/shard_map/psum | solution.py:13
  814.3 1.3 fusion.64
  815.7 188.3 %all-reduce.9 = (bf16[3456,256]{1,0:T(8,128)(2,1)}, bf16[3456,256]{0,1:T(8,128)(2,1)S(1)}, f32[3456]{0:T(1024)}) all-reduce(f32[3456,256]{1,0:T(8,128)} %get-tuple-element.151, f32[3456,256]{0,1:T(8,128)} %get-tuple-element.152, f32[3456]{0:T(1024)S(1)} %psum.62), channel_id=1, replica_groups=mesh['wide'=8,'narrow'=4] {'wide'}, use_global_device_ids=true, to_apply=%region_15.16 | all-reduce | flops 1772928 | bytes 10644480 | tf_op jit(solution)/shard_map/psum | solution.py:14
  1003.9 2.2 copy.35
  1006.2 3.5 multiply_reduce_fusion
  1009.7 4.3 divide_subtract_fusion
  (116 shorter events, 23.2 us)
Async XLA Ops:
  7.2 99.1 %copy-start = (bf16[3456,256]{1,0:T(8,128)(2,1)S(1)}, bf16[3456,256]{1,0:T(8,128)(2,1)}, u32[]{:S(2)}) copy-start(bf16[3456,256]{1,0:T(8,128)(2,1)} %param.19) | copy-start | bytes 5308420
  16.0 41.3 %copy-start.21 = (s32[144,26]{0,1:T(8,128)S(1)}, s32[144,26]{0,1:T(8,128)}, u32[]{:S(2)}) copy-start(s32[144,26]{0,1:T(8,128)} %param.29) | copy-start | bytes 44932
  57.6 46.7 %copy-start.2 = (bf16[144,3456]{1,0:T(8,128)(2,1)S(1)}, bf16[144,3456]{1,0:T(8,128)(2,1)}, u32[]{:S(2)}) copy-start(bf16[144,3456]{1,0:T(8,128)(2,1)} %param.17) | copy-start | bytes 2985988
  57.6 48.7 %copy-start.17 = (f32[3456]{0:T(1024)S(1)}, f32[3456]{0:T(1024)}, u32[]{:S(2)}) copy-start(f32[3456]{0:T(1024)} %param.22) | copy-start | bytes 41476
  57.6 48.7 %copy-start.22 = (f32[3456]{0:T(1024)S(1)}, f32[3456]{0:T(1024)}, u32[]{:S(2)}) copy-start(f32[3456]{0:T(1024)} %param.21) | copy-start | bytes 41476
  96.5 51.7 %all-to-all-start = ((s32[32,1,468]{2,1,0:T(1,128)}), s32[32,1,468]{2,1,0:T(1,128)S(1)}, u32[]{:S(2)}, u32[]{:S(2)}) async-start(s32[32,1,468]{2,1,0:T(1,128)} %all_to_all.11), calls=%async_computation | async-start | bytes 131072 | tf_op jit(solution)/shard_map/all_to_all | solution.py:86
  104.3 2.9 copy-start.26
  106.3 1.5 copy-start.9
  107.2 1.6 copy-start.5
  107.2 0.6 copy-start.23
  107.8 1.0 copy-start.12
  108.8 1.1 copy-start.11
  112.2 35.9 %copy-start.7 = (bf16[3744,128]{1,0:T(8,128)(2,1)}, bf16[3744,128]{1,0:T(8,128)(2,1)S(1)}, u32[]{:S(2)}) copy-start(bf16[3744,128]{1,0:T(8,128)(2,1)S(1)} %reshape.128) | copy-start | bytes 2875396
  148.1 6.9 copy-start.8
  148.1 0.6 copy-start.14
  148.8 299.6 %all-to-all-start.1 = ((bf16[32,468,128]{2,1,0:T(8,128)(2,1)}), bf16[32,468,128]{2,1,0:T(8,128)(2,1)}, u32[]{:S(2)}, u32[]{:S(2)}) async-start(bf16[32,468,128]{2,1,0:T(8,128)(2,1)} %reshape.134), calls=%async_computation.1 | async-start | bytes 7733248 | tf_op jit(solution)/shard_map/all_to_all | solution.py:79
  154.8 659.5 %all-reduce.8.cloned.1.call-start = ((), (), s32[]{:S(2)}) async-start(), calls=%async_computation.3 | async-start | bytes 22544384 | tf_op jit(solution)/shard_map/psum | solution.py:13
  155.1 267.2 %copy-start.3 = (bf16[144,3456]{1,0:T(8,128)(2,1)S(1)}, bf16[144,3456]{1,0:T(8,128)(2,1)}, u32[]{:S(2)}) copy-start(bf16[144,3456]{1,0:T(8,128)(2,1)} %param.17) | copy-start | bytes 2985988
  155.1 267.2 %copy-start.13 = (bf16[144,256]{1,0:T(8,128)(2,1)S(1)}, bf16[144,256]{1,0:T(8,128)(2,1)}, u32[]{:S(2)}) copy-start(bf16[144,256]{1,0:T(8,128)(2,1)} %copy-done.12) | copy-start | bytes 221188
  422.3 2.5 copy-start.10
  422.3 2.5 copy-start.18
  422.3 2.5 copy-start.24
  427.4 0.7 copy-start.19
  427.4 20.8 %copy-start.15 = (s32[32,1,468]{2,1,0:T(1,128)S(1)}, s32[32,1,468]{2,1,0:T(1,128)}, u32[]{:S(2)}) copy-start(s32[32,1,468]{2,1,0:T(1,128)} %copy-done.14) | copy-start | bytes 179716
  427.4 578.7 %all-reduce.6.cloned.1.call-start = ((), (), s32[]{:S(2)}) async-start(), calls=%async_computation.2 | async-start | bytes 8388608 | tf_op jit(solution)/shard_map/psum | solution.py:14
  448.2 6.0 copy-start.16
  454.2 58.3 %copy-start.25 = (f32[2048]{0:T(1024)S(1)}, f32[2048]{0:T(1024)}, u32[]{:S(2)}) copy-start(f32[2048]{0:T(1024)} %param.26) | copy-start | bytes 24580
  510.9 303.5 %copy-start.6 = (f32[2048,128]{1,0:T(8,128)S(1)}, f32[2048,128]{1,0:T(8,128)}, u32[]{:S(2)}) copy-start(f32[2048,128]{1,0:T(8,128)} %param.25) | copy-start | bytes 3145732
  1003.9 5.7 copy-start.20
  1006.1 3.5 copy-start.4
  1009.7 4.4 copy-start.1
Sparse Core Ops, SparseCore 0:
  427.5 386.7 all-reduce.7
  817.6 122.0 all-reduce.5
